TPU v7x, 32 devices: a whole 2x2x4 slice. The times are simulated.
32 devices in a mesh: pose: 2 (over y), grid: 8 (over z, x), depth: 2 (over core).
Axes of the slice: x: 2, y: 2, z: 4, core: 2. Of those that a mesh axis runs over, the one named last changes fastest.
Arguments:
- row_block: float32 [2048, 2048], P(('pose', 'grid'), 'depth'), parts along dimension 0, may hold values from -0.125 to 0.125
- column_block: float32 [4096, 12288], P(('pose', 'depth'), 'grid'), parts along dimension 0, may hold values from -6 to 6
- density_slab: float32 [2048, 12288], P(('pose', 'depth'), 'grid'), parts along dimension 0, may hold values from -6 to 6
Outputs:
- purified: float32 [2048, 12288], P(('pose', 'depth'), 'grid'), parts along dimension 0
There are 2 independent parts, one for each index of `pose`. A program takes and returns all parts, laid end to end along the dimension named above; each array names one. Nothing has to cross between parts.
All inputs are finite; a program needn't handle non-finite values.
Results may differ from a plain program's by a relative error of at most 0.00005.
Values sent between devices are 32-bit elements; how exact they have to be, the bound alone decides.
A program may use at most 64 MiB of HBM per device.

v0:
```python
import jax
import jax.numpy as jnp
from jax import lax
from jax.sharding import PartitionSpec as P


def multiply(left, right):
    return jnp.dot(left, right, preferred_element_type=jnp.float32, precision=lax.Precision.HIGHEST)


def local(row_block, column_block, density_slab):
    partial_slab = multiply(lax.all_gather(row_block, "grid", axis=0, tiled=True), column_block)
    squared = lax.psum_scatter(partial_slab, "depth", scatter_dimension=0, tiled=True)
    return 2.0 * density_slab - squared


def solution(mesh):
    placed = (
        P(("pose", "grid"), "depth"),
        P(("pose", "depth"), "grid"),
        P(("pose", "depth"), "grid"),
    )
    return jax.shard_map(
        local, mesh=mesh, in_specs=placed, out_specs=P(("pose", "depth"), "grid"), check_vma=False
    )
```

profile of v0, /device:TPU:0, one launch (start us, length us, event | category | flops | bytes accessed | tf_op | source)
XLA Modules:
  0.0 134.0 jit_solution(10082095884589365527)
XLA Ops:
  6.5 0.0 all-gather.2.cloned.1.call-start
  6.5 0.7 all-gather.2.cloned.1.call-update
  7.3 0.0 reduce-scatter.2.cloned.1.call-start
  7.3 78.3 %all-gather.2.cloned.1.call-done = f32[1024,1024]{1,0:T(8,128)} async-done(((f32[128,1024]{1,0:T(8,128)}), f32[1024,1024]{1,0:T(8,128)}) %all-gather.2.cloned.1.call-update) | async-done | bytes 4194320 | tf_op jit(solution)/shard_map/all_gather | solution.py:12
  85.6 24.4 %fusion = f32[1024,1536]{1,0:T(8,128)} fusion(f32[1024,1024]{1,0:T(8,128)} %all-gather.2.cloned.1.call-done, f32[1024,1536]{1,0:T(8,128)} %param.4), kind=kOutput, calls=%fused_computation.1 | convolution fusion | flops 19327352832 | bytes 16777216 | tf_op jit(solution)/shard_map/dot_general | solution.py:8
  110.0 0.0 copy-start
  110.0 0.0 reduce-scatter.2.cloned.1.call-update
  110.0 13.0 %reduce-scatter.2.cloned.1.call-done = f32[512,1536]{1,0:T(8,128)} async-done(((f32[1024,1536]{1,0:T(8,128)}), f32[512,1536]{1,0:T(8,128)}) %reduce-scatter.2.cloned.1.call-update) | async-done | bytes 3145744 | tf_op jit(solution)/shard_map/reduce_scatter | solution.py:13
  123.0 0.0 copy-done
  123.0 4.2 %multiply_subtract_fusion = f32[512,1536]{1,0:T(8,128)} fusion(f32[512,1536]{1,0:T(8,128)} %reduce-scatter.2.cloned.1.call-done, f32[512,1536]{1,0:T(8,128)S(1)} %copy-done), kind=kLoop, calls=%fused_computation | loop fusion | flops 1572864 | bytes 9437184 | tf_op jit(solution)/shard_map/sub | solution.py:14
Async XLA Ops:
  6.5 79.1 %all-gather.2.cloned.1.call-start = ((), (), s32[]{:S(2)}) async-start(), calls=%async_computation.1 | async-start | bytes 4718592 | tf_op jit(solution)/shard_map/all_gather | solution.py:12
  7.3 115.7 %reduce-scatter.2.cloned.1.call-start = ((), (), s32[]{:S(2)}) async-start(), calls=%async_computation.2 | async-start | bytes 9437184 | tf_op jit(solution)/shard_map/reduce_scatter | solution.py:13
  110.0 13.0 %copy-start = (f32[512,1536]{1,0:T(8,128)S(1)}, f32[512,1536]{1,0:T(8,128)}, u32[]{:S(2)}) copy-start(f32[512,1536]{1,0:T(8,128)} %param.5) | copy-start | bytes 9437188
Sparse Core Ops, SparseCore 0:
  9.5 76.0 all-gather.1
  110.2 12.7 reduce-scatter.1
where the time goes:
time: 134 us
  waiting for transfers between devices  92 us (69%)
  matrix products  24.4 us (18%)
  between operations  13.4 us (10%)
  other arithmetic  4.18 us (3%)
    all_gather x1, waiting for transfers between devices, local(): lax.all_gather(row_block, 'grid', axis=0, tiled=True)  78.3 us
    dot_general x1, matrix products, multiply(): jnp.dot(left, right, preferred_element_type=jnp.float32, precision=lax.Pr...  24.4 us
    reduce_scatter x1, waiting for transfers between devices, local(): lax.psum_scatter(partial_slab, 'depth', scatter_dimension=0, tiled=True)  13 us
    sub x1, other arithmetic, local(): return 2.0 * density_slab - squared  4.18 us
  transfers between devices with their start and end apart: 2, of which 2 were waited for; matrix products, arithmetic and copies ran while one was open for 0% of the time, Pallas kernels for 0%

commit v1 on v0

v1 whole, which is shorter than its diff:
```python
import functools

import jax
import jax.numpy as jnp
from jax import lax
from jax.experimental import pallas as pl
from jax.experimental.pallas import tpu as pltpu
from jax.sharding import PartitionSpec as P

MESH = pl.DeviceIdType.MESH
F32, BF16 = jnp.float32, jnp.bfloat16
TILE = 256


def split(value):
    high = value.astype(BF16)
    return high, (value - high.astype(F32)).astype(BF16)


def kernel(
    Z, X, C,
    a_hbm, b_hbm, d_hbm, o_hbm,
    a_all, b_raw, b_high, b_low, a_pair, share, other, slab, result,
    load_sem, b_sem, out_sem, zrecv, xrecv, zsend, xsend, crecv, csend,
):
    grid_at, core = lax.axis_index("grid"), lax.axis_index("depth")
    z, x = grid_at // X, grid_at % X
    G = Z * X
    half = G // 2
    R, K = a_hbm.shape
    N = b_hbm.shape[1]
    piece = R // C
    b_parts = b_sem.shape[0]
    b_rows = K // b_parts

    def rows_of(g):
        return pl.ds(pl.multiple_of(g * R, R), R)

    own_load = pltpu.make_async_copy(a_hbm, a_all.at[rows_of(grid_at)], load_sem.at[0])
    slab_load = pltpu.make_async_copy(d_hbm, slab, load_sem.at[1])
    own_load.start()
    b_loads = []
    for part in range(b_parts):
        rows = pl.ds(part * b_rows, b_rows)
        b_loads.append(pltpu.make_async_copy(b_hbm.at[rows], b_raw.at[rows], b_sem.at[part]))
        b_loads[-1].start()
    slab_load.start()

    barrier = pltpu.get_barrier_semaphore()

    @pl.when(z > 0)
    def _():
        pl.semaphore_signal(barrier, inc=1, device_id={"grid": grid_at - X}, device_id_type=MESH)

    @pl.when(z < Z - 1)
    def _():
        pl.semaphore_signal(barrier, inc=1, device_id={"grid": grid_at + X}, device_id_type=MESH)

    def beside(k):
        return z * X + lax.rem(x + k, X)

    for k in range(1, X):
        pl.semaphore_signal(barrier, inc=1, device_id={"grid": beside(k)}, device_id_type=MESH)
    pl.semaphore_signal(barrier, inc=1, device_id={"depth": 1 - core}, device_id_type=MESH)
    pl.semaphore_wait(barrier, X + (z > 0).astype(jnp.int32) + (z < Z - 1).astype(jnp.int32))

    def piece_rows(g, c):
        return pl.ds(pl.multiple_of(g * R + c * piece, piece), piece)

    def along_z(src, zb, c, step):
        way = 0 if step > 0 else 1
        return pltpu.make_async_remote_copy(
            src, a_all.at[piece_rows(zb * X + x, c)], zsend.at[way, zb], zrecv.at[zb, c],
            device_id={"grid": grid_at + step * X}, device_id_type=MESH)

    def along_x(src, zb, c, k):
        return pltpu.make_async_remote_copy(
            src, a_all.at[piece_rows(zb * X + x, c)], xsend.at[k - 1, zb], xrecv.at[zb * X + x],
            device_id={"grid": beside(k)}, device_id_type=MESH)

    for c in range(C):
        src = a_hbm.at[pl.ds(c * piece, piece)]

        @pl.when(z < Z - 1)
        def _():
            along_z(src, z, c, 1).start()

        @pl.when(z > 0)
        def _():
            along_z(src, z, c, -1).start()

        for k in range(1, X):
            along_x(src, z, c, k).start()

    def relay(d, c, step):
        zb = z - step * d

        @pl.when(jnp.logical_and(zb >= 0, zb < Z))
        def _():
            src = a_all.at[piece_rows(zb * X + x, c)]
            along_z(src, zb, c, step).wait_recv()
            onward = z + step

            @pl.when(jnp.logical_and(onward >= 0, onward < Z))
            def _():
                along_z(src, zb, c, step).start()

            for k in range(1, X):
                along_x(src, zb, c, k).start()

    def exchange(g):
        return pltpu.make_async_remote_copy(
            share.at[rows_of(g)], other.at[rows_of(lax.rem(g, half))],
            csend.at[lax.rem(g, half)], crecv.at[lax.rem(g, half)],
            device_id={"depth": 1 - core}, device_id_type=MESH)

    def compute(g):
        high, low = split(a_all[rows_of(g), :])
        a_pair[0:R, :] = high
        a_pair[R:2 * R, :] = low

        @pl.loop(0, N // TILE)
        def _(t):
            cols = pl.ds(pl.multiple_of(t * TILE, TILE), TILE)
            both = jnp.dot(a_pair[...], b_high[:, cols], preferred_element_type=F32)
            cross = jnp.dot(a_pair[0:R, :], b_low[:, cols], preferred_element_type=F32)
            share[rows_of(g), cols] = both[0:R] + (both[R:2 * R] + cross)

        @pl.when(g // half != core)
        def _():
            exchange(g).start()

    def put(g):
        rows = rows_of(lax.rem(g, half))
        return pltpu.make_async_copy(result.at[rows], o_hbm.at[rows], out_sem.at[lax.rem(g, half)])

    def finish(g):
        @pl.when(g // half == core)
        def _():
            exchange(g).wait_recv()
            rows = rows_of(lax.rem(g, half))
            result[rows, :] = 2.0 * slab[rows, :] - (share[rows_of(g), :] + other[rows, :])
            put(g).start()

    def site(d, j):
        k, up = j // 2, j % 2
        dist = d - (k > 0).astype(jnp.int32)
        zb = z + dist - 2 * dist * up
        fine = jnp.logical_and(jnp.logical_and(zb >= 0, zb < Z), jnp.logical_and(dist >= up, dist < Z))
        return zb * X + lax.rem(x + k, X), fine, k > 0

    def work(d):
        @pl.loop(0, 2 * X)
        def _(j):
            g, fine, came_x = site(d, j)

            @pl.when(fine)
            def _():
                @pl.when(came_x)
                def _():
                    pltpu.make_async_remote_copy(
                        a_all.at[rows_of(g)], a_all.at[rows_of(g)], xsend.at[0, 0], xrecv.at[g],
                        device_id={"grid": beside(1)}, device_id_type=MESH).wait_recv()

                compute(g)

    def conclude(d):
        @pl.loop(0, 2 * X)
        def _(j):
            g, fine, _ = site(d, j)

            @pl.when(fine)
            def _():
                finish(g)

    own_load.wait()
    for part in range(b_parts):
        b_loads[part].wait()

        @pl.loop(0, b_rows // 32)
        def _(i):
            rows = pl.ds(pl.multiple_of(part * b_rows + i * 32, 32), 32)
            high, low = split(b_raw[rows, :])
            b_high[rows, :] = high
            b_low[rows, :] = low

    slab_load.wait()
    compute(grid_at)

    @pl.loop(1, Z)
    def _(d):
        for c in range(C):
            relay(d, c, 1)
            relay(d, c, -1)
        work(d)

        @pl.when(d == 1)
        def _():
            finish(grid_at)

        @pl.when(d > 1)
        def _():
            conclude(d - 1)

    @pl.loop(0, Z)
    def _(zb):
        block = a_all.at[rows_of(zb * X + x)]

        def sent(sem, peer):
            pltpu.make_async_remote_copy(
                block, block, sem, xrecv.at[0], device_id={"grid": peer}, device_id_type=MESH).wait_send()

        @pl.when(jnp.logical_and(zb <= z, z < Z - 1))
        def _():
            sent(zsend.at[0, zb], grid_at + X)

        @pl.when(jnp.logical_and(zb >= z, z > 0))
        def _():
            sent(zsend.at[1, zb], grid_at - X)

    work(Z)
    conclude(Z - 1)
    conclude(Z)

    @pl.loop(0, Z)
    def _(zb):
        block = a_all.at[rows_of(zb * X + x)]
        for k in range(1, X):
            pltpu.make_async_remote_copy(
                block, block, xsend.at[k - 1, zb], xrecv.at[0],
                device_id={"grid": beside(k)}, device_id_type=MESH).wait_send()

    @pl.loop(0, half)
    def _(h):
        exchange((1 - core) * half + h).wait_send()
        put(core * half + h).wait()


def lines(grid):
    short = max(s for s in range(1, grid + 1) if grid % s == 0 and s * s * s <= grid)
    return grid // short, short


def local(Z, X, row_block, column_block, density_slab):
    (R, K), N = row_block.shape, column_block.shape[1]
    G, ROWS = Z * X, Z * X * R
    C = 4 if R % 32 == 0 else 1
    b_parts = 4
    dma = pltpu.SemaphoreType.DMA
    any_space = pl.BlockSpec(memory_space=pl.ANY)
    return pl.pallas_call(
        functools.partial(kernel, Z, X, C),
        out_shape=jax.ShapeDtypeStruct(density_slab.shape, F32),
        in_specs=[any_space] * 3,
        out_specs=any_space,
        scratch_shapes=[
            pltpu.VMEM((ROWS, K), F32),
            pltpu.VMEM((K, N), F32),
            pltpu.VMEM((K, N), BF16),
            pltpu.VMEM((K, N), BF16),
            pltpu.VMEM((2 * R, K), BF16),
            pltpu.VMEM((ROWS, N), F32),
            pltpu.VMEM((ROWS // 2, N), F32),
            pltpu.VMEM((ROWS // 2, N), F32),
            pltpu.VMEM((ROWS // 2, N), F32),
            dma((2,)),
            dma((b_parts,)),
            dma((G // 2,)),
            dma((Z, C)),
            dma((G,)),
            dma((2, Z)),
            dma((max(X - 1, 1), Z)),
            dma((G // 2,)),
            dma((G // 2,)),
        ],
        compiler_params=pltpu.CompilerParams(
            collective_id=0, has_side_effects=True, vmem_limit_bytes=48 * 2**20
        ),
        cost_estimate=pl.CostEstimate(
            flops=6 * ROWS * K * N, bytes_accessed=4 * (R * K + K * N + ROWS * N), transcendentals=0
        ),
    )(row_block, column_block, density_slab)


def solution(mesh):
    Z, X = lines(mesh.shape["grid"])
    placed = (
        P(("pose", "grid"), "depth"),
        P(("pose", "depth"), "grid"),
        P(("pose", "depth"), "grid"),
    )
    return jax.shard_map(
        functools.partial(local, Z, X), mesh=mesh, in_specs=placed, out_specs=P(("pose", "depth"), "grid"),
        check_vma=False,
    )
```

time: 134 us -> 57.8 us (0.43)
  waiting for transfers between devices: 92 us -> 0 us
  Pallas kernels: 0 us -> 54.7 us
  matrix products: 24.4 us -> 0 us
  between operations: 13.4 us -> 0.01 us
  other arithmetic: 4.18 us -> 0 us
  local copies, waits for them, and re-layouts: 0.01 us -> 2.71 us
    all_gather x1 -> x0, waiting for transfers between devices: 78.3 us -> none  [local(): lax.all_gather(row_block, 'grid', axis=0, tiled=True)]
    pallas_call x0 -> x1, Pallas kernels: none -> 54.7 us  [local(): pl.pallas_call(functools.partial(kernel, Z, X, C), out_shape=jax.ShapeDty...]
    dot_general x1 -> x0, matrix products: 24.4 us -> none  [multiply(): jnp.dot(left, right, preferred_element_type=jnp.float32, precision=lax.Pr...]
    reduce_scatter x1 -> x0, waiting for transfers between devices: 13 us -> none  [local(): lax.psum_scatter(partial_slab, 'depth', scatter_dimension=0, tiled=True)]
    sub x1 -> x0, other arithmetic: 4.18 us -> none  [local(): return 2.0 * density_slab - squared]
    unnamed x2 -> x3, local copies, waits for them, and re-layouts: 0.01 us -> 2.71 us
  transfers between devices with their start and end apart: 2 -> 0, of which waited for: 2 -> 0; matrix products, arithmetic and copies ran while one was open for 0% -> 0% of each run, Pallas kernels for 0% -> 0%
where the time goes in v1:
time: 57.8 us; the launch traced here: 57.4 us
  Pallas kernels  54.7 us (95%)
  local copies, waits for them, and re-layouts  2.71 us (5%)
    pallas_call x1, Pallas kernels, local(): pl.pallas_call(functools.partial(kernel, Z, X, C), out_shape=jax.ShapeDty...  54.7 us
    unnamed x3, local copies, waits for them, and re-layouts  2.71 us

profile of v1, /device:TPU:0, one launch (start us, length us, event | category | flops | bytes accessed | tf_op | source)
XLA Modules:
  0.0 57.4 jit_solution(15803988887915290481)
XLA Ops:
  0.0 0.0 copy-start
  0.0 1.0 %copy-done = f32[128,1024]{1,0:T(8,128)S(1)} copy-done((f32[128,1024]{1,0:T(8,128)S(1)}, f32[128,1024]{1,0:T(8,128)}, u32[]{:S(2)}) %copy-start) | copy-done | bytes 524312
  1.0 54.7 %shard_map.37 = f32[512,1536]{1,0:T(8,128)S(1)} custom-call(f32[128,1024]{1,0:T(8,128)S(1)} %copy-done, f32[1024,1536]{1,0:T(8,128)} %b_hbm.1, f32[512,1536]{1,0:T(8,128)} %d_hbm.1), custom_call_target="tpu_custom_call" | custom-call | flops 9663676416 | bytes 13107200 | tf_op jit(solution)/shard_map/pallas_call | solution.py:251
  55.8 1.7 %copy.5 = f32[512,1536]{1,0:T(8,128)} copy(f32[512,1536]{1,0:T(8,128)S(1)} %shard_map.37) | data formatting | bytes 6291456
Async XLA Ops:
  0.0 1.0 %copy-start = (f32[128,1024]{1,0:T(8,128)S(1)}, f32[128,1024]{1,0:T(8,128)}, u32[]{:S(2)}) copy-start(f32[128,1024]{1,0:T(8,128)} %a_hbm.1) | copy-start | bytes 1572868

commit v2 on v1

v2 whole, which is shorter than its diff:
```python
import functools

import jax
import jax.numpy as jnp
from jax import lax
from jax.experimental import pallas as pl
from jax.experimental.pallas import tpu as pltpu
from jax.sharding import PartitionSpec as P

MESH = pl.DeviceIdType.MESH
F32, BF16 = jnp.float32, jnp.bfloat16
TILE = 256


def split(value):
    high = value.astype(BF16)
    return high, (value - high.astype(F32)).astype(BF16)


def kernel(
    Z, X, far, pieces,
    a_hbm, b_hbm, d_hbm, result,
    a_all, b_raw, b_high, b_low, a_pair, share, other, slab,
    load_sem, b_sem, zrecv, xrecv, zsend, xsend, crecv, csend, far_recv, far_send,
):
    grid_at, core = lax.axis_index("grid"), lax.axis_index("depth")
    z, x = grid_at // X, grid_at % X
    G = Z * X
    half = G // 2
    R, K = a_hbm.shape
    N = b_hbm.shape[1]
    C = len(pieces)
    b_parts = b_sem.shape[0]
    b_rows = K // b_parts

    def rows_of(g):
        return pl.ds(pl.multiple_of(g * R, R), R)

    own_load = pltpu.make_async_copy(a_hbm, a_all.at[rows_of(grid_at)], load_sem.at[0])
    slab_load = pltpu.make_async_copy(d_hbm, slab, load_sem.at[1])
    own_load.start()
    b_loads = []
    for part in range(b_parts):
        rows = pl.ds(part * b_rows, b_rows)
        b_loads.append(pltpu.make_async_copy(b_hbm.at[rows], b_raw.at[rows], b_sem.at[part]))
        b_loads[-1].start()
    slab_load.start()

    barrier = pltpu.get_barrier_semaphore()

    @pl.when(z > 0)
    def _():
        pl.semaphore_signal(barrier, inc=1, device_id={"grid": grid_at - X}, device_id_type=MESH)

    @pl.when(z < Z - 1)
    def _():
        pl.semaphore_signal(barrier, inc=1, device_id={"grid": grid_at + X}, device_id_type=MESH)

    def beside(k):
        return z * X + lax.rem(x + k, X)

    for k in range(1, X):
        pl.semaphore_signal(barrier, inc=1, device_id={"grid": beside(k)}, device_id_type=MESH)
    pl.semaphore_signal(barrier, inc=1, device_id={"depth": 1 - core}, device_id_type=MESH)
    pl.semaphore_wait(barrier, X + (z > 0).astype(jnp.int32) + (z < Z - 1).astype(jnp.int32))

    def span(g, low, size):
        return pl.ds(pl.multiple_of(g * R + low, 8), size)

    def along_z(src, zb, c, step):
        way = 0 if step > 0 else 1
        k = max(c - C, 0)
        low, size = pieces[c] if c < C else (0, far)
        rows = span(zb * X + lax.rem(x + k, X), low, size)
        return pltpu.make_async_remote_copy(
            a_all.at[rows] if src is None else src, a_all.at[rows], zsend.at[way, zb], zrecv.at[zb, c],
            device_id={"grid": grid_at + step * X}, device_id_type=MESH)

    def along_x(src, zb, c, k):
        rows = span(zb * X + x, *pieces[c])
        return pltpu.make_async_remote_copy(
            a_all.at[rows] if src is None else src, a_all.at[rows], xsend.at[k - 1, zb], xrecv.at[zb * X + x, c],
            device_id={"grid": beside(k)}, device_id_type=MESH)

    def far_x(k):
        return pltpu.make_async_remote_copy(
            a_hbm.at[pl.ds(0, far)], a_all.at[span(grid_at, 0, far)], far_send.at[k - 1], far_recv.at[k - 1],
            device_id={"grid": beside(k)}, device_id_type=MESH)

    def both_ways(src, c):
        @pl.when(z < Z - 1)
        def _():
            along_z(src, z, c, 1).start()

        @pl.when(z > 0)
        def _():
            along_z(src, z, c, -1).start()

    if far:
        for k in range(1, X):
            far_x(k).start()
    for c in range(C):
        src = a_hbm.at[pl.ds(*pieces[c])]
        both_ways(src, c)
        for k in range(1, X):
            along_x(src, z, c, k).start()
    if far:
        both_ways(a_hbm.at[pl.ds(0, far)], C)

    def relay(d, c, step):
        zb = z - step * d

        @pl.when(jnp.logical_and(zb >= 0, zb < Z))
        def _():
            along_z(None, zb, c, step).wait_recv()
            onward = z + step

            @pl.when(jnp.logical_and(onward >= 0, onward < Z))
            def _():
                along_z(None, zb, c, step).start()

            if c < C:
                for k in range(1, X):
                    along_x(None, zb, c, k).start()

    def exchange(g, u=0, low=0, size=None):
        size = R if size is None else size
        h = lax.rem(g, half)
        return pltpu.make_async_remote_copy(
            share.at[span(g, low, size)], other.at[span(h, low, size)], csend.at[h], crecv.at[h, u],
            device_id={"depth": 1 - core}, device_id_type=MESH)

    def compute(g, u=0, low=0, size=None):
        size = R if size is None else size
        rows = span(g, low, size)
        top, rest = split(a_all[rows, :])
        a_pair[0:size, :] = top
        a_pair[size:2 * size, :] = rest

        @pl.loop(0, N // TILE)
        def _(t):
            cols = pl.ds(pl.multiple_of(t * TILE, TILE), TILE)
            both = jnp.dot(a_pair[0:2 * size, :], b_high[:, cols], preferred_element_type=F32)
            cross = jnp.dot(a_pair[0:size, :], b_low[:, cols], preferred_element_type=F32)
            share[rows, cols] = both[0:size] + (both[size:2 * size] + cross)

        @pl.when(g // half != core)
        def _():
            exchange(g, u, low, size).start()

    def finish(g, u=0, low=0, size=None):
        size = R if size is None else size

        @pl.when(g // half == core)
        def _():
            exchange(g, u, low, size).wait_recv()
            rows = span(lax.rem(g, half), low, size)
            result[rows, :] = 2.0 * slab[rows, :] - (share[span(g, low, size), :] + other[rows, :])

    def site(d, j):
        k, up = j // 2, j % 2
        dist = d - (k > 0).astype(jnp.int32)
        zb = z + dist - 2 * dist * up
        fine = jnp.logical_and(jnp.logical_and(zb >= 0, zb < Z), jnp.logical_and(dist >= up, dist < Z))
        return zb * X + lax.rem(x + k, X), fine, k > 0

    def arrived(g, c):
        rows = span(g, *pieces[c])
        pltpu.make_async_remote_copy(
            a_all.at[rows], a_all.at[rows], xsend.at[0, 0], xrecv.at[g, c],
            device_id={"grid": beside(1)}, device_id_type=MESH).wait_recv()

    def work(d):
        @pl.loop(0, 2 * X)
        def _(j):
            g, fine, came_x = site(d, j)

            @pl.when(fine)
            def _():
                @pl.when(came_x)
                def _():
                    for c in range(C):
                        arrived(g, c)

                compute(g)

    def conclude(d):
        @pl.loop(0, 2 * X)
        def _(j):
            g, fine, _ = site(d, j)

            @pl.when(fine)
            def _():
                finish(g)

    own_load.wait()
    for part in range(b_parts):
        b_loads[part].wait()

        @pl.loop(0, b_rows // 32)
        def _(i):
            rows = pl.ds(pl.multiple_of(part * b_rows + i * 32, 32), 32)
            high, low = split(b_raw[rows, :])
            b_high[rows, :] = high
            b_low[rows, :] = low

    if far:
        for k in range(1, X):
            g = beside(k)
            rows = span(g, 0, far)
            pltpu.make_async_remote_copy(
                a_all.at[rows], a_all.at[rows], far_send.at[0], far_recv.at[X - k - 1],
                device_id={"grid": g}, device_id_type=MESH).wait_recv()
            both_ways(None, C + k)
    compute(grid_at)
    slab_load.wait()

    @pl.loop(1, Z)
    def _(d):
        for c in range(C + X if far else C):
            relay(d, c, 1)
            relay(d, c, -1)
        work(d)

        @pl.when(d == 1)
        def _():
            finish(grid_at)

        @pl.when(d > 1)
        def _():
            conclude(d - 1)

    @pl.loop(0, Z)
    def _(zb):
        block = a_all.at[pl.ds(0, R + (X - 1) * far)]

        def sent(sem, peer):
            pltpu.make_async_remote_copy(
                block, block, sem, xrecv.at[0], device_id={"grid": peer}, device_id_type=MESH).wait_send()

        @pl.when(jnp.logical_and(zb <= z, z < Z - 1))
        def _():
            sent(zsend.at[0, zb], grid_at + X)

        @pl.when(jnp.logical_and(zb >= z, z > 0))
        def _():
            sent(zsend.at[1, zb], grid_at - X)

    cuts = sorted({low for low, _ in pieces[1:] if low % 16 == 0 and low * 2 >= R}) [:1]
    cuts = [0] + cuts + [R]
    units = [(u, low, high - low) for u, (low, high) in enumerate(zip(cuts, cuts[1:]))]

    def last(then):
        @pl.loop(2, 2 * X)
        def _(j):
            g, fine, _ = site(Z, j)

            @pl.when(fine)
            def _():
                then(g)

    def work_last(g):
        ready = 0
        for u, low, size in units:
            while ready < C and pieces[ready][0] < low + size:
                arrived(g, ready)
                ready += 1
            compute(g, u, low, size)

    def finish_last(g):
        for unit in units:
            finish(g, *unit)

    conclude(Z - 1)
    last(work_last)

    @pl.loop(0, Z)
    def _(zb):
        block = a_all.at[pl.ds(0, R - far)]
        for k in range(1, X):
            pltpu.make_async_remote_copy(
                block, block, xsend.at[k - 1, zb], xrecv.at[0, 0],
                device_id={"grid": beside(k)}, device_id_type=MESH).wait_send()

    if far:
        for k in range(1, X):
            far_x(k).wait_send()
    last(finish_last)

    @pl.loop(0, half)
    def _(h):
        exchange((1 - core) * half + h).wait_send()


def lines(grid):
    short = max(s for s in range(1, grid + 1) if grid % s == 0 and s * s * s <= grid)
    return grid // short, short


def local(Z, X, row_block, column_block, density_slab):
    (R, K), N = row_block.shape, column_block.shape[1]
    G, ROWS = Z * X, Z * X * R
    far = R * 3 // 16 // 8 * 8
    pieces = [(0, R)]
    if far:
        body = (R // 2 - far) // 8 * 8
        pieces = [(far, body), (R // 2, R // 4), (R // 2 + R // 4, R // 4)]
    C = len(pieces)
    b_parts = 4
    dma = pltpu.SemaphoreType.DMA
    far_space = pl.BlockSpec(memory_space=pltpu.HBM)
    return pl.pallas_call(
        functools.partial(kernel, Z, X, far, pieces),
        out_shape=pltpu.VMEM(density_slab.shape, F32),
        in_specs=[far_space] * 3,
        out_specs=pl.BlockSpec(memory_space=pltpu.VMEM),
        scratch_shapes=[
            pltpu.VMEM((ROWS, K), F32),
            pltpu.VMEM((K, N), F32),
            pltpu.VMEM((K, N), BF16),
            pltpu.VMEM((K, N), BF16),
            pltpu.VMEM((2 * R, K), BF16),
            pltpu.VMEM((ROWS, N), F32),
            pltpu.VMEM((ROWS // 2, N), F32),
            pltpu.VMEM((ROWS // 2, N), F32),
            dma((2,)),
            dma((b_parts,)),
            dma((Z, C + X)),
            dma((G, C)),
            dma((2, Z)),
            dma((max(X - 1, 1), Z)),
            dma((G // 2, 2)),
            dma((G // 2,)),
            dma((max(X - 1, 1),)),
            dma((max(X - 1, 1),)),
        ],
        compiler_params=pltpu.CompilerParams(
            collective_id=0, has_side_effects=True, vmem_limit_bytes=48 * 2**20
        ),
        cost_estimate=pl.CostEstimate(
            flops=6 * ROWS * K * N, bytes_accessed=4 * (R * K + K * N + ROWS * N), transcendentals=0
        ),
    )(*(pltpu.with_memory_space_constraint(each, pltpu.HBM) for each in (row_block, column_block, density_slab)))


def solution(mesh):
    Z, X = lines(mesh.shape["grid"])
    placed = (
        P(("pose", "grid"), "depth"),
        P(("pose", "depth"), "grid"),
        P(("pose", "depth"), "grid"),
    )
    return jax.shard_map(
        functools.partial(local, Z, X), mesh=mesh, in_specs=placed, out_specs=P(("pose", "depth"), "grid"),
        check_vma=False,
    )
```

time: 57.8 us -> 58.6 us (1.014)
  Pallas kernels: 54.7 us -> 56.3 us
  local copies, waits for them, and re-layouts: 2.71 us -> 1.67 us
    pallas_call x1, Pallas kernels: 54.7 us -> 56.3 us  [local(): pl.pallas_call(functools.partial(kernel, Z, X, far, pieces), out_shape=pl...]
    unnamed x3 -> x1, local copies, waits for them, and re-layouts: 2.71 us -> 1.67 us
where the time goes in v2:
time: 58.6 us; the launch traced here: 58 us
  Pallas kernels  56.3 us (96%)
  local copies, waits for them, and re-layouts  1.67 us (3%)
    pallas_call x1, Pallas kernels, local(): pl.pallas_call(functools.partial(kernel, Z, X, far, pieces), out_shape=pl...  56.3 us
    unnamed x1, local copies, waits for them, and re-layouts  1.67 us

profile of v2, /device:TPU:0, one launch (start us, length us, event | category | flops | bytes accessed | tf_op | source)
XLA Modules:
  0.0 58.0 jit_solution(15162433397351401202)
XLA Ops:
  0.0 56.3 %shard_map.37 = f32[512,1536]{1,0:T(8,128)S(1)} custom-call(f32[128,1024]{1,0:T(8,128)} %a_hbm.1, f32[1024,1536]{1,0:T(8,128)} %b_hbm.1, f32[512,1536]{1,0:T(8,128)} %d_hbm.1), custom_call_target="tpu_custom_call" | custom-call | flops 9663676416 | bytes 13107200 | tf_op jit(solution)/shard_map/pallas_call | solution.py:312
  56.3 1.7 %copy.5 = f32[512,1536]{1,0:T(8,128)} copy(f32[512,1536]{1,0:T(8,128)S(1)} %shard_map.37) | data formatting | bytes 6291456

commit v3 on v2

--- a/solution.py
+++ b/solution.py
@@ -9,7 +9,8 @@
 
 MESH = pl.DeviceIdType.MESH
 F32, BF16 = jnp.float32, jnp.bfloat16
-TILE = 256
+TILE = 768
+PIECE = 16
 
 
 def split(value):
@@ -18,7 +19,7 @@
 
 
 def kernel(
-    Z, X, far, pieces,
+    Z, X, far, S,
     a_hbm, b_hbm, d_hbm, result,
     a_all, b_raw, b_high, b_low, a_pair, share, other, slab,
     load_sem, b_sem, zrecv, xrecv, zsend, xsend, crecv, csend, far_recv, far_send,
@@ -29,7 +30,9 @@
     half = G // 2
     R, K = a_hbm.shape
     N = b_hbm.shape[1]
-    C = len(pieces)
+    C = (R - far) // PIECE
+    Q = R // 2 // PIECE
+    relayed = C + X if far else C
     b_parts = b_sem.shape[0]
     b_rows = K // b_parts
 
@@ -67,19 +70,21 @@
     def span(g, low, size):
         return pl.ds(pl.multiple_of(g * R + low, 8), size)
 
+    def low_of(c):
+        return jnp.where(c >= C, 0, jnp.where(c < Q, R - (Q - c) * PIECE, far + (c - Q) * PIECE))
+
     def along_z(src, zb, c, step):
         way = 0 if step > 0 else 1
-        k = max(c - C, 0)
-        low, size = pieces[c] if c < C else (0, far)
-        rows = span(zb * X + lax.rem(x + k, X), low, size)
+        rows = span(zb * X + lax.rem(x + jnp.maximum(c - C, 0), X), low_of(c), PIECE)
         return pltpu.make_async_remote_copy(
             a_all.at[rows] if src is None else src, a_all.at[rows], zsend.at[way, zb], zrecv.at[zb, c],
             device_id={"grid": grid_at + step * X}, device_id_type=MESH)
 
     def along_x(src, zb, c, k):
-        rows = span(zb * X + x, *pieces[c])
+        rows = span(zb * X + x, low_of(c), PIECE)
         return pltpu.make_async_remote_copy(
-            a_all.at[rows] if src is None else src, a_all.at[rows], xsend.at[k - 1, zb], xrecv.at[zb * X + x, c],
+            a_all.at[rows] if src is None else src, a_all.at[rows], xsend.at[k - 1, zb],
+            xrecv.at[zb * X + x, (c < Q).astype(jnp.int32)],
             device_id={"grid": beside(k)}, device_id_type=MESH)
 
     def far_x(k):
@@ -99,11 +104,13 @@
     if far:
         for k in range(1, X):
             far_x(k).start()
-    for c in range(C):
-        src = a_hbm.at[pl.ds(*pieces[c])]
+    @pl.loop(0, C)
+    def _(c):
+        src = a_hbm.at[pl.ds(pl.multiple_of(low_of(c), 8), PIECE)]
         both_ways(src, c)
         for k in range(1, X):
             along_x(src, z, c, k).start()
+
     if far:
         both_ways(a_hbm.at[pl.ds(0, far)], C)
 
@@ -119,7 +126,8 @@
             def _():
                 along_z(None, zb, c, step).start()
 
-            if c < C:
+            @pl.when(c < C)
+            def _():
                 for k in range(1, X):
                     along_x(None, zb, c, k).start()
 
@@ -157,41 +165,30 @@
             rows = span(lax.rem(g, half), low, size)
             result[rows, :] = 2.0 * slab[rows, :] - (share[span(g, low, size), :] + other[rows, :])
 
-    def site(d, j):
-        k, up = j // 2, j % 2
-        dist = d - (k > 0).astype(jnp.int32)
-        zb = z + dist - 2 * dist * up
-        fine = jnp.logical_and(jnp.logical_and(zb >= 0, zb < Z), jnp.logical_and(dist >= up, dist < Z))
-        return zb * X + lax.rem(x + k, X), fine, k > 0
-
-    def arrived(g, c):
-        rows = span(g, *pieces[c])
+    def arrived(g, u):
+        low, high = (R - Q * PIECE, R) if u else (far, R - Q * PIECE)
+        if low == high:
+            return
+        rows = span(g, low, high - low)
         pltpu.make_async_remote_copy(
-            a_all.at[rows], a_all.at[rows], xsend.at[0, 0], xrecv.at[g, c],
+            a_all.at[rows], a_all.at[rows], xsend.at[0, 0], xrecv.at[g, u],
             device_id={"grid": beside(1)}, device_id_type=MESH).wait_recv()
 
-    def work(d):
-        @pl.loop(0, 2 * X)
-        def _(j):
-            g, fine, came_x = site(d, j)
-
-            @pl.when(fine)
-            def _():
-                @pl.when(came_x)
-                def _():
-                    for c in range(C):
-                        arrived(g, c)
-
-                compute(g)
-
-    def conclude(d):
-        @pl.loop(0, 2 * X)
-        def _(j):
-            g, fine, _ = site(d, j)
-
-            @pl.when(fine)
-            def _():
-                finish(g)
+    def blocks(dist, down, first, end, then):
+        zb = z + dist - 2 * dist * down
+        fine = jnp.logical_and(jnp.logical_and(zb >= 0, zb < Z), jnp.logical_and(dist >= down, dist < Z))
+
+        @pl.loop(first, jnp.where(fine, end, first))
+        def _(k):
+            then(zb * X + lax.rem(x + k, X), k)
+
+    def full(g, k):
+        @pl.when(k > 0)
+        def _():
+            arrived(g, 1)
+            arrived(g, 0)
+
+        compute(g)
 
     own_load.wait()
     for part in range(b_parts):
@@ -212,85 +209,98 @@
                 a_all.at[rows], a_all.at[rows], far_send.at[0], far_recv.at[X - k - 1],
                 device_id={"grid": g}, device_id_type=MESH).wait_recv()
             both_ways(None, C + k)
-    compute(grid_at)
     slab_load.wait()
 
-    @pl.loop(1, Z)
-    def _(d):
-        for c in range(C + X if far else C):
+    @pl.loop(0, (Z - 1) * S + 5)
+    def _(s):
+        d, c = s // S + 1, s % S
+
+        @pl.when(jnp.logical_and(d < Z, c < relayed))
+        def _():
             relay(d, c, 1)
             relay(d, c, -1)
-        work(d)
-
-        @pl.when(d == 1)
-        def _():
-            finish(grid_at)
-
-        @pl.when(d > 1)
-        def _():
-            conclude(d - 1)
+
+        own = jnp.logical_or(c == 1, c == 2)
+        beyond = jnp.logical_or(c == 7, c == 8)
+        first = jnp.where(beyond, 1, 0)
+        end = jnp.where(beyond, X, jnp.where(own, 1, 0))
+        blocks(d - 1, jnp.where(beyond, c - 7, jnp.where(own, c - 1, 0)), first, end, full)
+
+        old = jnp.logical_or(c == 3, c == 4)
+        new = jnp.logical_or(c == 5, c == 6)
+        first = jnp.where(old, 1, 0)
+        end = jnp.where(old, X, jnp.where(new, 1, 0))
+
+        @pl.when(jnp.logical_or(jnp.logical_and(old, d > 1), new))
+        def _():
+            blocks(
+                jnp.where(old, d - 2, d - 1), jnp.where(old, c - 3, c - 5), first, end,
+                lambda g, k: finish(g))
+
+    parts = R // 2 // PIECE * PIECE * 2 == R and far > 0
+
+    def work_half(u):
+        def then(g, k):
+            arrived(g, u)
+            if parts:
+                compute(g, u, u * (R // 2), R // 2)
+            elif not u:
+                compute(g)
+
+        @pl.loop(0, 2)
+        def _(down):
+            blocks(Z - 1, down, 1, X, then)
+
+    def finish_half(u):
+        def then(g, k):
+            if parts:
+                finish(g, u, u * (R // 2), R // 2)
+            elif not u:
+                finish(g)
+
+        @pl.loop(0, 2)
+        def _(down):
+            blocks(Z - 1, down, 1, X, then)
+
+    work_half(1)
+
+    @pl.loop(0, 2)
+    def _(down):
+        blocks(Z - 1, down, 0, 1, lambda g, k: finish(g))
+
+    work_half(0)
+    finish_half(1)
 
     @pl.loop(0, Z)
     def _(zb):
         block = a_all.at[pl.ds(0, R + (X - 1) * far)]
-
-        def sent(sem, peer):
+        thin = a_all.at[pl.ds(0, R - far)]
+
+        def sent(block, sem, peer):
             pltpu.make_async_remote_copy(
-                block, block, sem, xrecv.at[0], device_id={"grid": peer}, device_id_type=MESH).wait_send()
+                block, block, sem, xrecv.at[0, 0], device_id={"grid": peer}, device_id_type=MESH).wait_send()
 
         @pl.when(jnp.logical_and(zb <= z, z < Z - 1))
         def _():
-            sent(zsend.at[0, zb], grid_at + X)
+            sent(block, zsend.at[0, zb], grid_at + X)
 
         @pl.when(jnp.logical_and(zb >= z, z > 0))
         def _():
-            sent(zsend.at[1, zb], grid_at - X)
-
-    cuts = sorted({low for low, _ in pieces[1:] if low % 16 == 0 and low * 2 >= R}) [:1]
-    cuts = [0] + cuts + [R]
-    units = [(u, low, high - low) for u, (low, high) in enumerate(zip(cuts, cuts[1:]))]
-
-    def last(then):
-        @pl.loop(2, 2 * X)
-        def _(j):
-            g, fine, _ = site(Z, j)
-
-            @pl.when(fine)
-            def _():
-                then(g)
-
-    def work_last(g):
-        ready = 0
-        for u, low, size in units:
-            while ready < C and pieces[ready][0] < low + size:
-                arrived(g, ready)
-                ready += 1
-            compute(g, u, low, size)
-
-    def finish_last(g):
-        for unit in units:
-            finish(g, *unit)
-
-    conclude(Z - 1)
-    last(work_last)
-
-    @pl.loop(0, Z)
-    def _(zb):
-        block = a_all.at[pl.ds(0, R - far)]
-        for k in range(1, X):
-            pltpu.make_async_remote_copy(
-                block, block, xsend.at[k - 1, zb], xrecv.at[0, 0],
-                device_id={"grid": beside(k)}, device_id_type=MESH).wait_send()
+            sent(block, zsend.at[1, zb], grid_at - X)
+
+        for k in range(1, X):
+            sent(thin, xsend.at[k - 1, zb], beside(k))
 
     if far:
         for k in range(1, X):
             far_x(k).wait_send()
-    last(finish_last)
 
     @pl.loop(0, half)
     def _(h):
         exchange((1 - core) * half + h).wait_send()
 
+    finish_half(0)
+
 
 def lines(grid):
     short = max(s for s in range(1, grid + 1) if grid % s == 0 and s * s * s <= grid)
@@ -300,17 +310,14 @@
 def local(Z, X, row_block, column_block, density_slab):
     (R, K), N = row_block.shape, column_block.shape[1]
     G, ROWS = Z * X, Z * X * R
-    far = R * 3 // 16 // 8 * 8
-    pieces = [(0, R)]
-    if far:
-        body = (R // 2 - far) // 8 * 8
-        pieces = [(far, body), (R // 2, R // 4), (R // 2 + R // 4, R // 4)]
-    C = len(pieces)
+    far = PIECE if R // PIECE >= 8 else 0
+    C = (R - far) // PIECE
+    S = max(C + X if far else C, 9)
     b_parts = 4
     dma = pltpu.SemaphoreType.DMA
     far_space = pl.BlockSpec(memory_space=pltpu.HBM)
     return pl.pallas_call(
-        functools.partial(kernel, Z, X, far, pieces),
+        functools.partial(kernel, Z, X, far, S),
         out_shape=pltpu.VMEM(density_slab.shape, F32),
         in_specs=[far_space] * 3,
         out_specs=pl.BlockSpec(memory_space=pltpu.VMEM),
@@ -325,8 +332,8 @@
             pltpu.VMEM((ROWS // 2, N), F32),
             dma((2,)),
             dma((b_parts,)),
-            dma((Z, C + X)),
-            dma((G, C)),
+            dma((Z, S)),
+            dma((G, 2)),
             dma((2, Z)),
             dma((max(X - 1, 1), Z)),
             dma((G // 2, 2)),

time: 58.6 us -> 52.9 us (0.903)
  Pallas kernels: 56.3 us -> 51.1 us
    pallas_call x1, Pallas kernels: 56.3 us -> 51.1 us  [local(): pl.pallas_call(functools.partial(kernel, Z, X, far, S), out_shape=pltpu.V...]
where the time goes in v3:
time: 52.9 us; the launch traced here: 52.8 us
  Pallas kernels  51.1 us (97%)
  local copies, waits for them, and re-layouts  1.67 us (3%)
    pallas_call x1, Pallas kernels, local(): pl.pallas_call(functools.partial(kernel, Z, X, far, S), out_shape=pltpu.V...  51.1 us
    unnamed x1, local copies, waits for them, and re-layouts  1.67 us

profile of v3, /device:TPU:0, one launch (start us, length us, event | category | flops | bytes accessed | tf_op | source)
XLA Modules:
  0.0 52.8 jit_solution(9561867772247422397)
XLA Ops:
  0.0 51.1 %shard_map.37 = f32[512,1536]{1,0:T(8,128)S(1)} custom-call(f32[128,1024]{1,0:T(8,128)} %a_hbm.1, f32[1024,1536]{1,0:T(8,128)} %b_hbm.1, f32[512,1536]{1,0:T(8,128)} %d_hbm.1), custom_call_target="tpu_custom_call" | custom-call | flops 9663676416 | bytes 13107200 | tf_op jit(solution)/shard_map/pallas_call | solution.py:319
  51.1 1.7 %copy.5 = f32[512,1536]{1,0:T(8,128)} copy(f32[512,1536]{1,0:T(8,128)S(1)} %shard_map.37) | data formatting | bytes 6291456

commit v4 on v3

--- a/solution.py
+++ b/solution.py
@@ -131,15 +131,16 @@
                 for k in range(1, X):
                     along_x(None, zb, c, k).start()
 
-    def exchange(g, u=0, low=0, size=None):
-        size = R if size is None else size
+    def tile(t):
+        return pl.ds(pl.multiple_of(t * TILE, TILE), TILE)
+
+    def exchange(g, u=0, low=0, size=R, cols=pl.ds(0, N)):
         h = lax.rem(g, half)
         return pltpu.make_async_remote_copy(
-            share.at[span(g, low, size)], other.at[span(h, low, size)], csend.at[h], crecv.at[h, u],
+            share.at[span(g, low, size), cols], other.at[span(h, low, size), cols], csend.at[h], crecv.at[h, u],
             device_id={"depth": 1 - core}, device_id_type=MESH)
 
-    def compute(g, u=0, low=0, size=None):
-        size = R if size is None else size
+    def compute(g, u=0, low=0, size=R):
         rows = span(g, low, size)
         top, rest = split(a_all[rows, :])
         a_pair[0:size, :] = top
@@ -147,23 +148,36 @@
 
         @pl.loop(0, N // TILE)
         def _(t):
-            cols = pl.ds(pl.multiple_of(t * TILE, TILE), TILE)
+            cols = tile(t)
             both = jnp.dot(a_pair[0:2 * size, :], b_high[:, cols], preferred_element_type=F32)
             cross = jnp.dot(a_pair[0:size, :], b_low[:, cols], preferred_element_type=F32)
             share[rows, cols] = both[0:size] + (both[size:2 * size] + cross)
-
-        @pl.when(g // half != core)
-        def _():
-            exchange(g, u, low, size).start()
-
-    def finish(g, u=0, low=0, size=None):
-        size = R if size is None else size
+            if size < R:
+                @pl.when(g // half != core)
+                def _():
+                    exchange(g, u * (N // TILE) + t, low, size, cols).start()
+
+        if size == R:
+            @pl.when(g // half != core)
+            def _():
+                exchange(g).start()
+
+    def finish(g, u=0, low=0, size=R):
+        rows = span(lax.rem(g, half), low, size)
+
+        def subtract(cols):
+            result[rows, cols] = 2.0 * slab[rows, cols] - (share[span(g, low, size), cols] + other[rows, cols])
 
         @pl.when(g // half == core)
         def _():
-            exchange(g, u, low, size).wait_recv()
-            rows = span(lax.rem(g, half), low, size)
-            result[rows, :] = 2.0 * slab[rows, :] - (share[span(g, low, size), :] + other[rows, :])
+            if size < R:
+                @pl.loop(0, N // TILE)
+                def _(t):
+                    exchange(g, u * (N // TILE) + t, low, size, tile(t)).wait_recv()
+                    subtract(tile(t))
+            else:
+                exchange(g).wait_recv()
+                subtract(slice(None))
 
     def arrived(g, u):
         low, high = (R - Q * PIECE, R) if u else (far, R - Q * PIECE)
@@ -211,11 +225,13 @@
             both_ways(None, C + k)
     slab_load.wait()
 
-    @pl.loop(0, (Z - 1) * S + 5)
+    reach = jnp.maximum(z, Z - 1 - z)
+
+    @pl.loop(0, reach * S + 5)
     def _(s):
         d, c = s // S + 1, s % S
 
-        @pl.when(jnp.logical_and(d < Z, c < relayed))
+        @pl.when(jnp.logical_and(d <= reach, c < relayed))
         def _():
             relay(d, c, 1)
             relay(d, c, -1)
@@ -249,7 +265,7 @@
 
         @pl.loop(0, 2)
         def _(down):
-            blocks(Z - 1, down, 1, X, then)
+            blocks(reach, down, 1, X, then)
 
     def finish_half(u):
         def then(g, k):
@@ -260,13 +276,13 @@
 
         @pl.loop(0, 2)
         def _(down):
-            blocks(Z - 1, down, 1, X, then)
+            blocks(reach, down, 1, X, then)
 
     work_half(1)
 
     @pl.loop(0, 2)
     def _(down):
-        blocks(Z - 1, down, 0, 1, lambda g, k: finish(g))
+        blocks(reach, down, 0, 1, lambda g, k: finish(g))
 
     work_half(0)
     finish_half(1)
@@ -336,7 +352,7 @@
             dma((G, 2)),
             dma((2, Z)),
             dma((max(X - 1, 1), Z)),
-            dma((G // 2, 2)),
+            dma((G // 2, 2 * N // TILE)),
             dma((G // 2,)),
             dma((max(X - 1, 1),)),
             dma((max(X - 1, 1),)),

time: 52.9 us -> 52.7 us (level)
  no operation moved by 1% of the time
where the time goes in v4:
time: 52.7 us; the launch traced here: 52.6 us
  Pallas kernels  50.9 us (97%)
  local copies, waits for them, and re-layouts  1.67 us (3%)
    pallas_call x1, Pallas kernels, local(): pl.pallas_call(functools.partial(kernel, Z, X, far, S), out_shape=pltpu.V...  50.9 us
    unnamed x1, local copies, waits for them, and re-layouts  1.67 us

profile of v4, /device:TPU:0, one launch (start us, length us, event | category | flops | bytes accessed | tf_op | source)
XLA Modules:
  0.0 52.6 jit_solution(9120515224292546984)
XLA Ops:
  0.0 50.9 %shard_map.37 = f32[512,1536]{1,0:T(8,128)S(1)} custom-call(f32[128,1024]{1,0:T(8,128)} %a_hbm.1, f32[1024,1536]{1,0:T(8,128)} %b_hbm.1, f32[512,1536]{1,0:T(8,128)} %d_hbm.1), custom_call_target="tpu_custom_call" | custom-call | flops 9663676416 | bytes 13107200 | tf_op jit(solution)/shard_map/pallas_call | solution.py:335
  50.9 1.7 %copy.5 = f32[512,1536]{1,0:T(8,128)} copy(f32[512,1536]{1,0:T(8,128)S(1)} %shard_map.37) | data formatting | bytes 6291456

commit v5 on v4

--- a/solution.py
+++ b/solution.py
@@ -9,7 +9,7 @@
 
 MESH = pl.DeviceIdType.MESH
 F32, BF16 = jnp.float32, jnp.bfloat16
-TILE = 768
+TILE = 1536
 PIECE = 16
 
 

time: 52.7 us -> 51.9 us (0.985)
  Pallas kernels: 50.9 us -> 50.1 us
    pallas_call x1, Pallas kernels: 50.9 us -> 50.1 us  [local(): pl.pallas_call(functools.partial(kernel, Z, X, far, S), out_shape=pltpu.V...]
where the time goes in v5:
time: 51.9 us; the launch traced here: 51.7 us
  Pallas kernels  50.1 us (97%)
  local copies, waits for them, and re-layouts  1.67 us (3%)
    pallas_call x1, Pallas kernels, local(): pl.pallas_call(functools.partial(kernel, Z, X, far, S), out_shape=pltpu.V...  50.1 us
    unnamed x1, local copies, waits for them, and re-layouts  1.67 us

profile of v5, /device:TPU:0, one launch (start us, length us, event | category | flops | bytes accessed | tf_op | source)
XLA Modules:
  0.0 51.7 jit_solution(3714866231062577214)
XLA Ops:
  0.0 50.1 %shard_map.37 = f32[512,1536]{1,0:T(8,128)S(1)} custom-call(f32[128,1024]{1,0:T(8,128)} %a_hbm.1, f32[1024,1536]{1,0:T(8,128)} %b_hbm.1, f32[512,1536]{1,0:T(8,128)} %d_hbm.1), custom_call_target="tpu_custom_call" | custom-call | flops 9663676416 | bytes 13107200 | tf_op jit(solution)/shard_map/pallas_call | solution.py:335
  50.1 1.7 %copy.5 = f32[512,1536]{1,0:T(8,128)} copy(f32[512,1536]{1,0:T(8,128)S(1)} %shard_map.37) | data formatting | bytes 6291456
